TPU v7x, 256 devices: a whole 4x4x8 slice. The times are simulated.
256 devices in a mesh: ctx: 128 (over x, z, y), head: 2 (over core).
Axes of the slice: x: 4, y: 4, z: 8, core: 2. Of those that a mesh axis runs over, the one named last changes fastest.
Arguments:
- queries: bfloat16 [16384, 256], P('ctx', 'head'), may hold values from -100 to 100
- keys: bfloat16 [16384, 256], P('ctx', 'head'), may hold values from -5 to 5
- values: bfloat16 [16384, 256], P('ctx', 'head'), may hold values from -6 to 6
- picks: int32 [2, 128, 2], P('head'), may hold values from 0 to 6, as said below
- out_weight: bfloat16 [256, 4096], P('head'), may hold values from -0.375 to 0.375
Outputs:
- mixed: bfloat16 [16384, 4096], P('ctx', 'head')
Inputs may be any that keep to these rules, and one draw needn't show every extreme that they name: `picks`: an entry not below its block's own span (b * 128 // 2048 for block b) is ignored; where the own span is 2 or more, both entries of a block are below it and differ.
All inputs are finite; a program needn't handle non-finite values.
Results may differ from a plain program's by a relative error of at most 0.012.
Values may be sent and summed in bfloat16 or wider, within the bound.
A program may use at most 64 MiB of HBM per device.

v0:
```python
import math

import jax
import jax.numpy as jnp
from jax import lax
from jax.sharding import PartitionSpec as P

SPAN = 2048
QBLK = 128


NEGATIVE = -1e30


def local(queries, keys, values, picks, out_weight):
    tok_rows = queries.shape[0]
    width = queries.shape[1]
    local_heads = picks.shape[0]
    head_dim = width // local_heads
    anchor = lax.axis_index("ctx") * tok_rows
    scale = 1.0 / math.sqrt(head_dim)
    per_span = SPAN // QBLK
    gathered = lax.all_gather(queries, "ctx", axis=0, tiled=True)
    groups = gathered.shape[0] // SPAN
    key_local = keys.reshape(tok_rows, local_heads, head_dim)
    value_local = values.reshape(tok_rows, local_heads, head_dim)
    key_pos = anchor + jnp.arange(tok_rows, dtype=jnp.int32)
    key_span = anchor // SPAN

    def group_scores(group):
        rows = lax.dynamic_slice_in_dim(gathered, group * SPAN, SPAN, 0)
        rows = rows.reshape(SPAN, local_heads, head_dim)
        scores = (
            jnp.einsum("thd,shd->ths", rows, key_local, preferred_element_type=jnp.float32) * scale
        )
        query_pos = group * SPAN + jnp.arange(SPAN, dtype=jnp.int32)
        chosen_rows = lax.dynamic_slice_in_dim(picks, group * per_span, per_span, 1)
        chosen_rows = jnp.repeat(chosen_rows, QBLK, axis=1)
        first = chosen_rows[:, :, 0].T
        second = chosen_rows[:, :, 1].T
        own = (key_span == group) & (key_pos[None, :] <= query_pos[:, None])
        chosen = ((first == key_span) | (second == key_span)) & (key_span < group)
        valid = own[:, None, :] | chosen[:, :, None]
        return (scores, valid)

    def local_top(group):
        scores, valid = group_scores(group)
        return jnp.max(jnp.where(valid, scores, NEGATIVE), axis=2)

    group_ids = jnp.arange(groups, dtype=jnp.int32)
    local_max = lax.map(local_top, group_ids).reshape(groups * SPAN, local_heads)
    row_max = lax.pmax(local_max, "ctx")

    def partial_terms(item):
        group, top = item
        scores, valid = group_scores(group)
        weights = jnp.exp(jnp.where(valid, scores - top[:, :, None], NEGATIVE))
        total = jnp.sum(weights, axis=2)
        numer = jnp.einsum(
            "ths,shd->thd",
            weights.astype(jnp.bfloat16),
            value_local,
            preferred_element_type=jnp.float32,
        )
        return (numer.reshape(SPAN, local_heads * head_dim), total)

    numer_all, total_all = lax.map(
        partial_terms, (group_ids, row_max.reshape(groups, SPAN, local_heads))
    )
    numer_all = numer_all.reshape(groups * SPAN, local_heads * head_dim)
    total_all = total_all.reshape(groups * SPAN, local_heads)
    numer, total = (
        lax.psum_scatter(numer_all, "ctx", scatter_dimension=0, tiled=True),
        lax.psum_scatter(total_all, "ctx", scatter_dimension=0, tiled=True),
    )
    attended = numer.reshape(tok_rows, local_heads, head_dim) / total[:, :, None]
    attended = attended.reshape(tok_rows, width).astype(jnp.bfloat16)
    term = jnp.dot(attended, out_weight, preferred_element_type=jnp.float32)
    mixed = lax.psum_scatter(term.astype(jnp.bfloat16), "head", scatter_dimension=1, tiled=True)
    return mixed


def solution(mesh):
    placed = (
        P("ctx", "head"),
        P("ctx", "head"),
        P("ctx", "head"),
        P("head", None, None),
        P("head", None),
    )
    return jax.shard_map(
        local, mesh=mesh, in_specs=placed, out_specs=P("ctx", "head"), check_vma=False
    )
```

profile of v0, /device:TPU:3, one launch (start us, length us, event | category | flops | bytes accessed | tf_op | source)
XLA Modules:
  0.0 1878.1 jit_solution(12322711171719957501)
XLA Ops:
  7.3 119.7 %all-gather.2.cloned.1.call-done = bf16[16384,128]{1,0:T(8,128)(2,1)} async-done(((bf16[128,128]{1,0:T(8,128)(2,1)}), bf16[16384,128]{1,0:T(8,128)(2,1)}) %all-gather.2.cloned.1.call-update) | async-done | bytes 4194320 | tf_op jit(solution)/shard_map/all_gather | solution.py:23
  127.1 43.7 %while.24 = (s32[]{:T(128)}, f32[8,2048,1]{1,2,0:T(1,128)S(1)}, s32[8]{0:T(128)S(1)}, s32[]{:T(128)}, s32[1,128,2]{1,2,0:T(2,128)}, /*index=5*/bf16[16384,128]{1...) while((s32[]{:T(128)}, f32[8,2048,1]{1,2,0:T(1,128)S(1)}, ...), condition=%wide.region_2.3_spmd.clone, body=%wide.region_0.2_spmd.clone.sunk | while | flops 68690056 | bytes 669345 | solution.py:51
  131.0 1.5 fusion.36
  136.5 1.5 fusion.36
  141.9 1.5 fusion.36
  147.4 1.5 fusion.36
  152.9 1.5 fusion.36
  158.3 1.5 fusion.36
  169.2 1.5 fusion.36
  171.5 205.8 %all-reduce.2.cloned.1.call-done = f32[8,2048,1]{1,2,0:T(1,128)} async-done(((f32[8,2048,1]{1,2,0:T(1,128)}), f32[8,2048,1]{1,2,0:T(1,128)}) %all-reduce.2.cloned.1.call-update) | async-done | bytes 65552 | tf_op jit(solution)/shard_map/pmax | solution.py:52
  377.3 61.9 %while.25 = (s32[]{:T(128)}, f32[8,2048,128]{2,1,0:T(8,128)}, f32[8,2048,1]{1,2,0:T(1,128)S(1)}, s32[8]{0:T(128)S(1)}, s32[]{:T(128)}, /*index=5*/s32[1,128,2]{1...) while((s32[]{:T(128)}, f32[8,2048,128]{2,1,0:T(8,128)}, ...), condition=%wide.region_6.7_spmd.clone, body=%wide.region_4.6_spmd.clone.sunk | while | flops 136323200 | bytes 2823873 | solution.py:67
  382.1 1.6 fusion.40
  389.8 1.6 fusion.40
  397.6 1.6 fusion.40
  405.3 1.6 fusion.40
  413.0 1.6 fusion.40
  420.7 1.6 fusion.40
  428.5 1.6 fusion.40
  436.2 1.6 fusion.40
  439.2 4.9 copy.8
  444.7 539.9 %reduce-scatter.10.cloned.1.call-done = f32[128,1]{1,0:T(8,128)} async-done(((f32[16384,1]{1,0:T(8,128)}), f32[128,1]{1,0:T(8,128)}) %reduce-scatter.10.cloned.1.call-update) | async-done | bytes 528
  985.6 702.1 %reduce-scatter.6.cloned.1.call-done = f32[128,128]{1,0:T(8,128)} async-done(((f32[16384,128]{1,0:T(8,128)}), f32[128,128]{1,0:T(8,128)}) %reduce-scatter.6.cloned.1.call-update) | async-done | bytes 65552 | tf_op jit(solution)/shard_map/reduce_scatter | solution.py:73
  1687.6 2.3 convolution_convert_fusion
  1690.0 181.6 %reduce-scatter.8.cloned.1.call-done = bf16[128,2048]{1,0:T(8,128)(2,1)} async-done(((bf16[128,4096]{1,0:T(8,128)(2,1)}), bf16[128,2048]{1,0:T(8,128)(2,1)}) %reduce-scatter.8.cloned.1.call-update) | async-done | bytes 524304 | tf_op jit(solution)/shard_map/reduce_scatter | solution.py:79
  (167 shorter events, 44.9 us)
Async XLA Ops:
  6.5 1681.1 %copy-start = (bf16[128,4096]{1,0:T(8,128)(2,1)S(1)}, bf16[128,4096]{1,0:T(8,128)(2,1)}, u32[]{:S(2)}) copy-start(bf16[128,4096]{1,0:T(8,128)(2,1)} %param.13) | copy-start | bytes 3145732
  6.5 370.7 %copy-start.1 = (bf16[128,128]{1,0:T(8,128)(2,1)S(1)}, bf16[128,128]{1,0:T(8,128)(2,1)}, u32[]{:S(2)}) copy-start(bf16[128,128]{1,0:T(8,128)(2,1)} %param.11) | copy-start | bytes 98308
  6.5 120.5 %all-gather.2.cloned.1.call-start = ((), (), s32[]{:S(2)}) async-start(), calls=%async_computation.3 | async-start | bytes 4227072 | tf_op jit(solution)/shard_map/all_gather | solution.py:23
  7.3 370.0 %all-reduce.2.cloned.1.call-start = ((), (), s32[]{:S(2)}) async-start(), calls=%async_computation.4 | async-start | bytes 131072 | tf_op jit(solution)/shard_map/pmax | solution.py:52
  170.7 0.6 copy-start.2
  171.4 813.3 %reduce-scatter.10.cloned.1.call-start = ((), (), s32[]{:S(2)}) async-start(), calls=%async_computation.7 | async-start | bytes 8454144
  444.1 1243.5 %reduce-scatter.6.cloned.1.call-start = ((), (), s32[]{:S(2)}) async-start(), calls=%async_computation.5 | async-start | bytes 8454144 | tf_op jit(solution)/shard_map/reduce_scatter | solution.py:73
  444.7 1426.9 %reduce-scatter.8.cloned.1.call-start = ((), (), s32[]{:S(2)}) async-start(), calls=%async_computation.6 | async-start | bytes 1572864 | tf_op jit(solution)/shard_map/reduce_scatter | solution.py:79
Sparse Core Ops, SparseCore 0:
  11.0 115.9 all-gather.1
  171.5 205.6 all-reduce.1
  444.2 540.3 reduce-scatter.9
  987.2 700.4 reduce-scatter.5
  1690.1 181.4 reduce-scatter.7
where the time goes:
time: 1880 us
  waiting for transfers between devices  1750 us (93%)
  loops' own time  40.6 us (2%)
  matrix products  37.6 us (2%)
  local copies, waits for them, and re-layouts  35.3 us (2%)
    reduce_scatter x1, waiting for transfers between devices, local(): lax.psum_scatter(numer_all, 'ctx', scatter_dimension=0, tiled=True)  702 us
    unnamed x6, waiting for transfers between devices  541 us
    pmax x1, waiting for transfers between devices, local(): row_max = lax.pmax(local_max, 'ctx')  206 us
    reduce_scatter x1, waiting for transfers between devices, local(): lax.psum_scatter(term.astype(jnp.bfloat16), 'head', scatter_dimension=1,...  182 us
    all_gather x1, waiting for transfers between devices, local(): gathered = lax.all_gather(queries, 'ctx', axis=0, tiled=True)  120 us
  transfers between devices with their start and end apart: 5, of which 5 were waited for; matrix products, arithmetic and copies ran while one was open for 0% of the time, Pallas kernels for 0%

commit v1 on v0

v1 whole, which is shorter than its diff:
```python
import functools
import math

import jax
import jax.numpy as jnp
from jax import lax
from jax.experimental import pallas as pl
from jax.experimental.pallas import tpu as pltpu
from jax.sharding import PartitionSpec as P

BLK = 128
SPANS = 8
ZN = 4
YN = 4
GROUP = ZN * YN
CHUNK = YN * BLK
COLS = 2048
NEGATIVE = -1e30
RATE = math.log2(math.e) / math.sqrt(128.0)
MESH = pl.DeviceIdType.MESH


def kernel(
    q_hbm, k_hbm, v_hbm, picks_hbm, w_hbm, out_ref,
    picks, kbuf, vbuf, qbuf, vraw, pout, sout, pin, sin, wbuf, att, top, total, acc,
    local_sem, z_send, z_recv, y_send, y_recv, q_send, q_recv, p_send, p_recv, h_send, h_recv,
):
    ctx = lax.axis_index("ctx")
    head = lax.axis_index("head")
    span = ctx // GROUP
    z = (ctx % GROUP) // YN
    y = ctx % YN
    right, left = (y + 1) % YN, (y + YN - 1) % YN
    z_peer = [z, z + 1 - 2 * (z % 2), (z + 2) % ZN, ZN - 1 - z]
    other = 1 - head

    def device(to_span, to_z, to_y):
        return (to_span * GROUP + to_z * YN + to_y, head)

    def remote(src, dst, send, recv, to):
        return pltpu.make_async_remote_copy(
            src_ref=src, dst_ref=dst, send_sem=send, recv_sem=recv, device_id=to, device_id_type=MESH
        )

    mine = [
        pltpu.make_async_copy(v_hbm, vraw, local_sem.at[0]),
        pltpu.make_async_copy(k_hbm, kbuf.at[0, y], local_sem.at[1]),
        pltpu.make_async_copy(q_hbm, qbuf.at[0], local_sem.at[2]),
        pltpu.make_async_copy(
            w_hbm.at[:, pl.ds(pl.multiple_of(head * COLS, COLS), COLS)], wbuf.at[0], local_sem.at[3]
        ),
        pltpu.make_async_copy(picks_hbm, picks, local_sem.at[4]),
    ]
    for copy in mine:
        copy.start()

    barrier = pltpu.get_barrier_semaphore()
    greeted = [device(span, z_peer[i], y) for i in range(1, ZN)]
    greeted += [device(span, z, right), device(span, z, left)]
    greeted += [device((span + d) % SPANS, z, y) for d in range(1, SPANS)]
    greeted += [(ctx, other)]
    for peer in greeted:
        pl.semaphore_signal(barrier, inc=1, device_id=peer, device_id_type=MESH)

    for v in range(1, SPANS):
        @pl.when(span + v >= SPANS)
        def _():
            qbuf[v] = jnp.zeros((BLK, BLK), jnp.bfloat16)

    mine[0].wait()
    vbuf[0, y] = vraw[...].T
    mine[1].wait()
    mine[2].wait()
    pl.semaphore_wait(barrier, len(greeted))

    def z_copy(i, which):
        buf = (kbuf, vbuf)[which]
        return remote(
            buf.at[0, y], buf.at[i, y], z_send.at[i, which], z_recv.at[i, which], device(span, z_peer[i], y)
        )

    def y_copies(i):
        at_right, at_left = device(span, z, right), device(span, z, left)
        return [
            remote(kbuf.at[i, y], kbuf.at[i, y], y_send.at[i, 0], y_recv.at[i, 0], at_right),
            remote(vbuf.at[i, y], vbuf.at[i, y], y_send.at[i, 3], y_recv.at[i, 3], at_left),
            remote(kbuf.at[i, y], kbuf.at[i, y], y_send.at[i, 1], y_recv.at[i, 1], at_left),
            remote(vbuf.at[i, y], vbuf.at[i, y], y_send.at[i, 2], y_recv.at[i, 2], at_right),
        ]

    def relays(i):
        return [
            remote(
                kbuf.at[i, left], kbuf.at[i, left], y_send.at[i, 4], y_recv.at[i, 4], device(span, z, right)
            ),
            remote(
                vbuf.at[i, right], vbuf.at[i, right], y_send.at[i, 5], y_recv.at[i, 5], device(span, z, left)
            ),
        ]

    def q_copy(v):
        return remote(
            qbuf.at[0], qbuf.at[v], q_send.at[v], q_recv.at[v], device((span + SPANS - v) % SPANS, z, y)
        )

    def p_copies(v):
        home = device((span + v) % SPANS, z, y)
        return [
            remote(pout.at[v], pin.at[v], p_send.at[v, 0], p_recv.at[v, 0], home),
            remote(sout.at[v], sin.at[v], p_send.at[v, 1], p_recv.at[v, 1], home),
        ]

    w_copy = remote(
        w_hbm.at[:, pl.ds(pl.multiple_of(other * COLS, COLS), COLS)],
        wbuf.at[1], h_send.at[0], h_recv.at[0], (ctx, other),
    )
    att_copy = remote(att.at[0], att.at[1], h_send.at[1], h_recv.at[1], (ctx, other))

    def spread(i):
        if i:
            z_copy(i, 0).wait_recv()
            z_copy(i, 1).wait_recv()
        for copy in y_copies(i):
            copy.start()

    def pass_on(i):
        from_near = y_copies(i)
        onward = relays(i)
        from_near[0].wait_recv()
        onward[0].start()
        from_near[1].wait_recv()
        onward[1].start()

    def arrive(i):
        from_near = y_copies(i)
        from_near[2].wait_recv()
        from_near[3].wait_recv()
        for copy in relays(i):
            copy.wait_recv()

    def attend(i, p, masked):
        queries = qbuf[pl.ds(2 * p, 2)].reshape(2 * BLK, BLK)
        keys = kbuf[i].reshape(CHUNK, BLK)
        scores = lax.dot_general(
            keys, queries, (((1,), (1,)), ((), ())), preferred_element_type=jnp.float32
        )
        if masked:
            key = lax.broadcasted_iota(jnp.int32, (CHUNK, 2 * BLK), 0)
            token = lax.broadcasted_iota(jnp.int32, (CHUNK, 2 * BLK), 1)
            if i == 0:
                last = y * BLK + token
            else:
                last = jnp.where(z_peer[i] < z, CHUNK, -1)
            allowed = (token >= BLK) | (key <= last)
            scores = jnp.where(allowed, scores, NEGATIVE)
        high = jnp.max(scores, axis=0, keepdims=True)
        if i:
            high = jnp.maximum(high, top[p])
        weights = jnp.exp2((scores - high) * RATE)
        part = jnp.sum(weights, axis=0, keepdims=True)
        values = jnp.concatenate([vbuf[i, b] for b in range(YN)], axis=1)
        numer = jnp.dot(values, weights.astype(jnp.bfloat16), preferred_element_type=jnp.float32)
        if i:
            fade = jnp.exp2((top[p] - high) * RATE)
            part = part + total[p] * fade
            numer = numer + acc[p] * fade
        top[p] = high
        total[p] = part
        acc[p] = numer

    def finish(p):
        for side in range(2):
            v = 2 * p + side
            lanes = slice(side * BLK, (side + 1) * BLK)

            @pl.when((v >= 1) & (span + v < SPANS))
            def _():
                part = total[p, :, lanes]
                pout[v] = (acc[p, :, lanes] / part).astype(jnp.bfloat16)
                sout[v, 0:4] = jnp.broadcast_to(top[p, :, lanes], (4, BLK))
                sout[v, 4:8] = jnp.broadcast_to(part, (4, BLK))
                for copy in p_copies(v):
                    copy.start()

    pairs = (SPANS - span + 1) // 2

    def compute(i):
        arrive(i)
        attend(i, 0, True)
        if i == ZN - 1:
            finish(0)

        def body(p, carry):
            attend(i, p, False)
            if i == ZN - 1:
                finish(p)
            return carry

        lax.fori_loop(1, pairs, body, 0)

    z_copy(1, 0).start()
    z_copy(1, 1).start()
    spread(0)
    for i in range(2, ZN):
        z_copy(i, 0).start()
        z_copy(i, 1).start()
    for v in range(1, SPANS):
        @pl.when(span >= v)
        def _():
            q_copy(v).start()
    w_copy.start()
    pass_on(0)
    spread(1)
    for v in range(1, SPANS):
        @pl.when(span + v < SPANS)
        def _():
            q_copy(v).wait_recv()
    compute(0)
    for i in range(1, ZN):
        pass_on(i)
        if i + 1 < ZN:
            spread(i + 1)
        compute(i)

    mine[4].wait()
    def gather(u, carry):
        for copy in p_copies(u):
            copy.wait_recv()
        which = span - u
        picked = (picks[0, 0, ctx] == which) | (picks[0, 1, ctx] == which)
        theirs = jnp.where(picked, sin[u, 0:1], NEGATIVE)
        ours = top[0, :, 0:BLK]
        high = jnp.maximum(ours, theirs)
        fade = jnp.exp2((ours - high) * RATE)
        share = sin[u, 4:5] * jnp.exp2((theirs - high) * RATE)
        top[0, :, 0:BLK] = high
        total[0, :, 0:BLK] = total[0, :, 0:BLK] * fade + share
        acc[0, :, 0:BLK] = acc[0, :, 0:BLK] * fade + pin[u].astype(jnp.float32) * share
        return carry

    lax.fori_loop(1, span + 1, gather, 0)
    att[0] = (acc[0, :, 0:BLK] / total[0, :, 0:BLK]).T.astype(jnp.bfloat16)
    att_copy.start()
    mine[3].wait()
    w_copy.wait_recv()
    att_copy.wait_recv()
    attended = jnp.concatenate([att[0], att[1]], axis=1)
    wide = 512

    def project(n, carry):
        columns = pl.ds(pl.multiple_of(n * wide, wide), wide)
        weight = wbuf[:, :, columns].reshape(2 * BLK, wide)
        out_ref[:, columns] = jnp.dot(attended, weight, preferred_element_type=jnp.float32).astype(jnp.bfloat16)
        return carry

    lax.fori_loop(0, COLS // wide, project, 0)

    for i in range(ZN):
        if i:
            z_copy(i, 0).wait_send()
            z_copy(i, 1).wait_send()
        for copy in y_copies(i) + relays(i):
            copy.wait_send()
    for v in range(1, SPANS):
        @pl.when(span >= v)
        def _():
            q_copy(v).wait_send()

        @pl.when(span + v < SPANS)
        def _():
            for copy in p_copies(v):
                copy.wait_send()
    w_copy.wait_send()
    att_copy.wait_send()


def local(queries, keys, values, picks, out_weight):
    hbm = pl.BlockSpec(memory_space=pltpu.HBM)
    dma = pltpu.SemaphoreType.DMA
    bf16, f32 = jnp.bfloat16, jnp.float32
    return pl.pallas_call(
        kernel,
        out_shape=jax.ShapeDtypeStruct((BLK, COLS), bf16),
        in_specs=[hbm] * 5,
        out_specs=pl.BlockSpec(memory_space=pltpu.VMEM),
        scratch_shapes=[
            pltpu.SMEM((1, 2, BLK), jnp.int32),
            pltpu.VMEM((ZN, YN, BLK, BLK), bf16),
            pltpu.VMEM((ZN, YN, BLK, BLK), bf16),
            pltpu.VMEM((SPANS, BLK, BLK), bf16),
            pltpu.VMEM((BLK, BLK), bf16),
            pltpu.VMEM((SPANS, BLK, BLK), bf16),
            pltpu.VMEM((SPANS, 8, BLK), f32),
            pltpu.VMEM((SPANS, BLK, BLK), bf16),
            pltpu.VMEM((SPANS, 8, BLK), f32),
            pltpu.VMEM((2, BLK, COLS), bf16),
            pltpu.VMEM((2, BLK, BLK), bf16),
            pltpu.VMEM((SPANS // 2, 1, 2 * BLK), f32),
            pltpu.VMEM((SPANS // 2, 1, 2 * BLK), f32),
            pltpu.VMEM((SPANS // 2, BLK, 2 * BLK), f32),
            dma((5,)),
            dma((ZN, 2)),
            dma((ZN, 2)),
            dma((ZN, 6)),
            dma((ZN, 6)),
            dma((SPANS,)),
            dma((SPANS,)),
            dma((SPANS, 2)),
            dma((SPANS, 2)),
            dma((2,)),
            dma((2,)),
        ],
        compiler_params=pltpu.CompilerParams(
            collective_id=0, has_side_effects=True, vmem_limit_bytes=56 * 1024 * 1024
        ),
        cost_estimate=pl.CostEstimate(flops=2**30, bytes_accessed=2**22, transcendentals=2**21),
    )(queries, keys, values, jnp.swapaxes(picks, 1, 2), out_weight)


def solution(mesh):
    placed = (
        P("ctx", "head"),
        P("ctx", "head"),
        P("ctx", "head"),
        P("head", None, None),
        P("head", None),
    )
    return jax.shard_map(
        local, mesh=mesh, in_specs=placed, out_specs=P("ctx", "head"), check_vma=False
    )
```

time: 1880 us -> 54.6 us (0.03)
  the two profiles are of different devices: /device:TPU:3 before, /device:TPU:7 now
where the time goes in v1:
time: 54.6 us; the launch traced here: 54.5 us
  Pallas kernels  52.6 us (96%)
  local copies, waits for them, and re-layouts  1.88 us (3%)
    pallas_call x1, Pallas kernels, local(): pl.pallas_call(kernel, out_shape=jax.ShapeDtypeStruct((BLK, COLS), bf16),...  52.6 us
    unnamed x1, local copies, waits for them, and re-layouts  1.88 us

profile of v1, /device:TPU:7, one launch (start us, length us, event | category | flops | bytes accessed | tf_op | source)
XLA Modules:
  0.0 54.5 jit_solution(7258822165581219342)
XLA Ops:
  0.0 52.6 %shard_map.55 = bf16[128,2048]{1,0:T(8,128)(2,1)} custom-call(bf16[128,128]{1,0:T(8,128)(2,1)} %q_hbm.1, bf16[128,128]{1,0:T(8,128)(2,1)} %k_hbm.1, bf16[128,128]{1,0:T(8,128)(2,1)} %v_hbm.1, s32[1,2,128]{2,1,0:T(2,128)} %bitcast.1, bf16[128,4096]{1,0:T(8,128)(2,1)} %w_hbm.1), custom_call_target="tpu_custom_call" | custom-call | flops 1073741824 | bytes 4194304 | tf_op jit(solution)/shard_map/pallas_call | solution.py:281
  52.6 1.9 %copy.7 = bf16[128,2048]{1,0:T(8,128)(2,1)} copy(bf16[128,2048]{1,0:T(8,128)(2,1)} %shard_map.55) | data formatting | bytes 1048576

commit v2 on v1

v2 whole, which is shorter than its diff:
```python
import math

import jax
import jax.numpy as jnp
from jax import lax
from jax.experimental import pallas as pl
from jax.experimental.pallas import tpu as pltpu
from jax.sharding import PartitionSpec as P

BLK = 128
XN = 4
YN = 4
MATES = 4
SLOTS = XN * MATES
CHUNK = YN * BLK
COLS = 2048
NEGATIVE = -1e30
RATE = math.log2(math.e) / math.sqrt(128.0)
MESH = pl.DeviceIdType.MESH


def kernel(
    q_hbm, k_hbm, v_hbm, picks_hbm, w_hbm, out_ref,
    picks, kv, qbuf, vraw, pout, sout, pin, sin, wbuf, att, top, total, acc,
    x_sem, local_sem, kv_send, kv_recv, q_send, q_recv, p_send, p_recv, h_send, h_recv,
):
    ctx = lax.axis_index("ctx")
    head = lax.axis_index("head")
    x = ctx // 32
    z = (ctx % 32) // 4
    y = ctx % 4
    half = z // 4
    low = z % 4
    span = 2 * x + half
    pair_z = z + 1 - 2 * (z % 2)
    across = z - low + (low + 2) % 4
    mate_z = [z, across, 7 - z, 7 - across]
    other = 1 - head

    def device(to_x, to_z, to_y):
        return (to_x * 32 + to_z * 4 + to_y, head)

    def remote(src, dst, send, recv, to):
        return pltpu.make_async_remote_copy(
            src_ref=src, dst_ref=dst, send_sem=send, recv_sem=recv, device_id=to, device_id_type=MESH
        )

    mine = [
        pltpu.make_async_copy(v_hbm, vraw, local_sem.at[0]),
        pltpu.make_async_copy(k_hbm, kv.at[0, y, pl.ds(0, BLK)], local_sem.at[1]),
        pltpu.make_async_copy(q_hbm, qbuf.at[0], local_sem.at[2]),
        pltpu.make_async_copy(
            w_hbm.at[:, pl.ds(pl.multiple_of(head * COLS, COLS), COLS)], wbuf.at[0], local_sem.at[3]
        ),
        pltpu.make_async_copy(picks_hbm, picks, local_sem.at[4]),
    ]
    row_peers = [(d, device(x, z, (y + d) % YN)) for d in range(1, YN)]
    pair_peers = [(d, device(x, pair_z, (y + d) % YN)) for d in range(YN)]
    x_peers = [device((x + d) % XN, z, y) for d in range(1, XN)]
    greeted = [to for _, to in row_peers + pair_peers]
    greeted += [device(x, mate_z[k], y) for k in range(1, MATES)] + x_peers + [(ctx, other)]
    barrier = pltpu.get_barrier_semaphore()
    for to in greeted:
        pl.semaphore_signal(barrier, inc=1, device_id=to, device_id_type=MESH)
    for copy in mine:
        copy.start()

    @pl.when(low >= 2)
    def _():
        qbuf[1] = jnp.zeros((BLK, BLK), jnp.bfloat16)

    mine[0].wait()
    kv[0, y, BLK:] = vraw[...].T
    mine[1].wait()
    mine[2].wait()
    pl.semaphore_wait(barrier, len(greeted))
    for to in x_peers:
        pl.semaphore_signal(x_sem, inc=1, device_id=to, device_id_type=MESH)

    def row_copy(d, to):
        return remote(kv.at[0, y], kv.at[0, y], kv_send.at[0, d], kv_recv.at[0, d], to)

    def pair_copy(d, to):
        return remote(kv.at[0, y], kv.at[1, y], kv_send.at[1, d], kv_recv.at[1, d], to)

    def q_copy(dx, k):
        slot = dx * MATES + k
        to = device((x + XN - dx) % XN, mate_z[k], y)
        return remote(qbuf.at[0], qbuf.at[slot], q_send.at[slot], q_recv.at[slot], to)

    def p_copies(slot, to):
        return [
            remote(pout.at[slot], pin.at[slot], p_send.at[slot, 0], p_recv.at[slot, 0], to),
            remote(sout.at[slot], sin.at[slot], p_send.at[slot, 1], p_recv.at[slot, 1], to),
        ]

    def visits(dx, k):
        if dx:
            return x >= dx
        return low >= 2 if k == 1 else half == 1

    def hosts(dx, k):
        if dx:
            return x + dx < XN
        return low < 2 if k == 1 else half == 0

    w_copy = remote(
        w_hbm.at[:, pl.ds(pl.multiple_of(other * COLS, COLS), COLS)],
        wbuf.at[1], h_send.at[0], h_recv.at[0], (ctx, other),
    )
    att_copy = remote(att.at[0], att.at[1], h_send.at[1], h_recv.at[1], (ctx, other))

    for d, to in row_peers:
        row_copy(d, to).start()
    for d, to in pair_peers:
        pair_copy(d, to).start()
    near = [(dx, 0) for dx in range(1, XN)] + [(0, k) for k in range(1, MATES)]
    far = [(dx, k) for dx in range(1, XN) for k in range(1, MATES)]
    for dx, k in near:
        @pl.when(visits(dx, k))
        def _():
            q_copy(dx, k).start()
    pl.semaphore_wait(x_sem, len(x_peers))
    for dx, k in far:
        @pl.when(visits(dx, k))
        def _():
            q_copy(dx, k).start()
    w_copy.start()

    def attend(i, p, masked):
        queries = qbuf[pl.ds(2 * p, 2)].reshape(2 * BLK, BLK)
        keys = kv[i, :, 0:BLK].reshape(CHUNK, BLK)
        scores = lax.dot_general(
            keys, queries, (((1,), (1,)), ((), ())), preferred_element_type=jnp.float32
        )
        if masked:
            key = lax.broadcasted_iota(jnp.int32, (CHUNK, 2 * BLK), 0)
            token = lax.broadcasted_iota(jnp.int32, (CHUNK, 2 * BLK), 1)
            if i == 0:
                last = y * BLK + token
            else:
                last = jnp.where(pair_z < z, CHUNK, -1)
            allowed = (token >= BLK) | (key <= last)
            scores = jnp.where(allowed, scores, NEGATIVE)
        high = jnp.max(scores, axis=0, keepdims=True)
        if i:
            high = jnp.maximum(high, top[p])
        weights = jnp.exp2((scores - high) * RATE)
        part = jnp.sum(weights, axis=0, keepdims=True)
        values = jnp.concatenate([kv[i, b, BLK:] for b in range(YN)], axis=1)
        numer = jnp.dot(values, weights.astype(jnp.bfloat16), preferred_element_type=jnp.float32)
        if i:
            fade = jnp.exp2((top[p] - high) * RATE)
            part = part + total[p] * fade
            numer = numer + acc[p] * fade
        top[p] = high
        total[p] = part
        acc[p] = numer

    def give_back(p, side, slot, to):
        lanes = slice(side * BLK, (side + 1) * BLK)
        part = total[p, :, lanes]
        pout[slot] = (acc[p, :, lanes] / part).astype(jnp.bfloat16)
        sout[slot, 0:4] = jnp.broadcast_to(top[p, :, lanes], (4, BLK))
        sout[slot, 4:8] = jnp.broadcast_to(part, (4, BLK))
        for copy in p_copies(slot, to):
            copy.start()

    first, ends = 1 + half, 2 * (XN - x)

    def compute(i):
        def body(n, carry):
            p = ends - 1 - n
            attend(i, p, False)
            if i:
                for side in range(2):
                    straight = mate_z[side]
                    to_z = straight + (p % 2) * (7 - 2 * straight)
                    give_back(p, side, 2 * p + side, device(x + p // 2, to_z, y))
            return carry

        lax.fori_loop(0, ends - first, body, 0)
        attend(i, 0, True)
        if i:
            @pl.when(low < 2)
            def _():
                give_back(0, 1, 1, device(x, across, y))

    for d, to in row_peers:
        row_copy(d, to).wait_recv()
    for dx, k in near + far:
        @pl.when(hosts(dx, k))
        def _():
            q_copy(dx, k).wait_recv()
    compute(0)
    for d, to in pair_peers:
        pair_copy(d, to).wait_recv()
    compute(1)

    mine[4].wait()
    first_pick, second_pick = picks[0, 0, ctx], picks[0, 1, ctx]
    for dx, k in [(0, 1), (0, 2), (0, 3)] + [(dx, k) for dx in (1, 3, 2) for k in range(MATES)]:
        @pl.when(visits(dx, k))
        def _():
            slot = dx * MATES + k
            for copy in p_copies(slot, (ctx, head)):
                copy.wait_recv()
            theirs = sin[slot, 0:1]
            if (dx, k) != (0, 1):
                which = 2 * (x - dx) + (half if k < 2 else 1 - half)
                picked = (first_pick == which) | (second_pick == which)
                theirs = jnp.where(picked, theirs, NEGATIVE)
            ours = top[0, :, 0:BLK]
            high = jnp.maximum(ours, theirs)
            fade = jnp.exp2((ours - high) * RATE)
            share = sin[slot, 4:5] * jnp.exp2((theirs - high) * RATE)
            top[0, :, 0:BLK] = high
            total[0, :, 0:BLK] = total[0, :, 0:BLK] * fade + share
            acc[0, :, 0:BLK] = acc[0, :, 0:BLK] * fade + pin[slot].astype(jnp.float32) * share

    att[0] = (acc[0, :, 0:BLK] / total[0, :, 0:BLK]).T.astype(jnp.bfloat16)
    att_copy.start()
    mine[3].wait()
    w_copy.wait_recv()
    att_copy.wait_recv()
    attended = jnp.concatenate([att[0], att[1]], axis=1)
    wide = 512

    def project(n, carry):
        columns = pl.ds(pl.multiple_of(n * wide, wide), wide)
        weight = wbuf[:, :, columns].reshape(2 * BLK, wide)
        out_ref[:, columns] = jnp.dot(attended, weight, preferred_element_type=jnp.float32).astype(jnp.bfloat16)
        return carry

    lax.fori_loop(0, COLS // wide, project, 0)

    for d, to in row_peers:
        row_copy(d, to).wait_send()
    for d, to in pair_peers:
        pair_copy(d, to).wait_send()
    for dx, k in near + far:
        @pl.when(visits(dx, k))
        def _():
            q_copy(dx, k).wait_send()

        @pl.when(hosts(dx, k))
        def _():
            for copy in p_copies(dx * MATES + k, device((x + dx) % XN, mate_z[k], y)):
                copy.wait_send()
    w_copy.wait_send()
    att_copy.wait_send()


def local(queries, keys, values, picks, out_weight):
    hbm = pl.BlockSpec(memory_space=pltpu.HBM)
    dma = pltpu.SemaphoreType.DMA
    bf16, f32 = jnp.bfloat16, jnp.float32
    return pl.pallas_call(
        kernel,
        out_shape=jax.ShapeDtypeStruct((BLK, COLS), bf16),
        in_specs=[hbm] * 5,
        out_specs=pl.BlockSpec(memory_space=pltpu.VMEM),
        scratch_shapes=[
            pltpu.SMEM((1, 2, BLK), jnp.int32),
            pltpu.VMEM((2, YN, 2 * BLK, BLK), bf16),
            pltpu.VMEM((SLOTS, BLK, BLK), bf16),
            pltpu.VMEM((BLK, BLK), bf16),
            pltpu.VMEM((SLOTS, BLK, BLK), bf16),
            pltpu.VMEM((SLOTS, 8, BLK), f32),
            pltpu.VMEM((SLOTS, BLK, BLK), bf16),
            pltpu.VMEM((SLOTS, 8, BLK), f32),
            pltpu.VMEM((2, BLK, COLS), bf16),
            pltpu.VMEM((2, BLK, BLK), bf16),
            pltpu.VMEM((SLOTS // 2, 1, 2 * BLK), f32),
            pltpu.VMEM((SLOTS // 2, 1, 2 * BLK), f32),
            pltpu.VMEM((SLOTS // 2, BLK, 2 * BLK), f32),
            pltpu.SemaphoreType.REGULAR,
            dma((5,)),
            dma((2, YN)),
            dma((2, YN)),
            dma((SLOTS,)),
            dma((SLOTS,)),
            dma((SLOTS, 2)),
            dma((SLOTS, 2)),
            dma((2,)),
            dma((2,)),
        ],
        compiler_params=pltpu.CompilerParams(
            collective_id=0, has_side_effects=True, vmem_limit_bytes=56 * 1024 * 1024
        ),
        cost_estimate=pl.CostEstimate(flops=2**30, bytes_accessed=2**22, transcendentals=2**21),
    )(queries, keys, values, jnp.swapaxes(picks, 1, 2), out_weight)


def solution(mesh):
    placed = (
        P("ctx", "head"),
        P("ctx", "head"),
        P("ctx", "head"),
        P("head", None, None),
        P("head", None),
    )
    return jax.shard_map(
        local, mesh=mesh, in_specs=placed, out_specs=P("ctx", "head"), check_vma=False
    )
```

time: 54.6 us -> 46.1 us (0.84)
  the two profiles are of different devices: /device:TPU:7 before, /device:TPU:3 now
where the time goes in v2:
time: 46.1 us; the launch traced here: 45.8 us
  Pallas kernels  43.9 us (95%)
  local copies, waits for them, and re-layouts  1.88 us (4%)
    pallas_call x1, Pallas kernels, local(): pl.pallas_call(kernel, out_shape=jax.ShapeDtypeStruct((BLK, COLS), bf16),...  43.9 us
    unnamed x1, local copies, waits for them, and re-layouts  1.88 us

profile of v2, /device:TPU:3, one launch (start us, length us, event | category | flops | bytes accessed | tf_op | source)
XLA Modules:
  0.0 45.8 jit_solution(15962246910869268829)
XLA Ops:
  0.0 43.9 %shard_map.55 = bf16[128,2048]{1,0:T(8,128)(2,1)} custom-call(bf16[128,128]{1,0:T(8,128)(2,1)} %q_hbm.1, bf16[128,128]{1,0:T(8,128)(2,1)} %k_hbm.1, bf16[128,128]{1,0:T(8,128)(2,1)} %v_hbm.1, s32[1,2,128]{2,1,0:T(2,128)} %bitcast.1, bf16[128,4096]{1,0:T(8,128)(2,1)} %w_hbm.1), custom_call_target="tpu_custom_call" | custom-call | flops 1073741824 | bytes 4194304 | tf_op jit(solution)/shard_map/pallas_call | solution.py:258
  43.9 1.9 %copy.7 = bf16[128,2048]{1,0:T(8,128)(2,1)} copy(bf16[128,2048]{1,0:T(8,128)(2,1)} %shard_map.55) | data formatting | bytes 1048576

commit v3 on v2

--- a/solution.py
+++ b/solution.py
@@ -69,6 +69,10 @@
     def _():
         qbuf[1] = jnp.zeros((BLK, BLK), jnp.bfloat16)
 
+    @pl.when(half == 1)
+    def _():
+        qbuf[2:4] = jnp.zeros((2, BLK, BLK), jnp.bfloat16)
+
     mine[0].wait()
     kv[0, y, BLK:] = vraw[...].T
     mine[1].wait()
@@ -114,8 +118,8 @@
         row_copy(d, to).start()
     for d, to in pair_peers:
         pair_copy(d, to).start()
-    near = [(dx, 0) for dx in range(1, XN)] + [(0, k) for k in range(1, MATES)]
-    far = [(dx, k) for dx in range(1, XN) for k in range(1, MATES)]
+    near = [(0, k) for k in range(1, MATES)] + [(dx, 0) for dx in (2, 3, 1)]
+    far = [(dx, k) for dx in (2, 3, 1) for k in range(1, MATES)]
     for dx, k in near:
         @pl.when(visits(dx, k))
         def _():
@@ -127,98 +131,95 @@
             q_copy(dx, k).start()
     w_copy.start()
 
-    def attend(i, p, masked):
-        queries = qbuf[pl.ds(2 * p, 2)].reshape(2 * BLK, BLK)
-        keys = kv[i, :, 0:BLK].reshape(CHUNK, BLK)
+    def attend(dx):
+        queries = qbuf[pl.ds(dx * MATES, MATES)].reshape(MATES * BLK, BLK)
+        keys = jnp.concatenate([kv[i, :, 0:BLK].reshape(CHUNK, BLK) for i in range(2)], axis=0)
         scores = lax.dot_general(
             keys, queries, (((1,), (1,)), ((), ())), preferred_element_type=jnp.float32
         )
-        if masked:
-            key = lax.broadcasted_iota(jnp.int32, (CHUNK, 2 * BLK), 0)
-            token = lax.broadcasted_iota(jnp.int32, (CHUNK, 2 * BLK), 1)
-            if i == 0:
-                last = y * BLK + token
-            else:
-                last = jnp.where(pair_z < z, CHUNK, -1)
-            allowed = (token >= BLK) | (key <= last)
-            scores = jnp.where(allowed, scores, NEGATIVE)
+        if dx == 0:
+            key = lax.broadcasted_iota(jnp.int32, (2 * CHUNK, BLK), 0)
+            token = lax.broadcasted_iota(jnp.int32, (2 * CHUNK, BLK), 1)
+            last = jnp.where(key < CHUNK, y * BLK + token, jnp.where(pair_z < z, 2 * CHUNK, -1))
+            own = jnp.where(key <= last, scores[:, 0:BLK], NEGATIVE)
+            scores = jnp.concatenate([own, scores[:, BLK:]], axis=1)
         high = jnp.max(scores, axis=0, keepdims=True)
-        if i:
-            high = jnp.maximum(high, top[p])
         weights = jnp.exp2((scores - high) * RATE)
         part = jnp.sum(weights, axis=0, keepdims=True)
-        values = jnp.concatenate([kv[i, b, BLK:] for b in range(YN)], axis=1)
+        values = jnp.concatenate([kv[i, b, BLK:] for i in range(2) for b in range(YN)], axis=1)
         numer = jnp.dot(values, weights.astype(jnp.bfloat16), preferred_element_type=jnp.float32)
-        if i:
-            fade = jnp.exp2((top[p] - high) * RATE)
-            part = part + total[p] * fade
-            numer = numer + acc[p] * fade
-        top[p] = high
-        total[p] = part
-        acc[p] = numer
-
-    def give_back(p, side, slot, to):
-        lanes = slice(side * BLK, (side + 1) * BLK)
-        part = total[p, :, lanes]
-        pout[slot] = (acc[p, :, lanes] / part).astype(jnp.bfloat16)
-        sout[slot, 0:4] = jnp.broadcast_to(top[p, :, lanes], (4, BLK))
-        sout[slot, 4:8] = jnp.broadcast_to(part, (4, BLK))
-        for copy in p_copies(slot, to):
-            copy.start()
-
-    first, ends = 1 + half, 2 * (XN - x)
-
-    def compute(i):
-        def body(n, carry):
-            p = ends - 1 - n
-            attend(i, p, False)
-            if i:
-                for side in range(2):
-                    straight = mate_z[side]
-                    to_z = straight + (p % 2) * (7 - 2 * straight)
-                    give_back(p, side, 2 * p + side, device(x + p // 2, to_z, y))
-            return carry
-
-        lax.fori_loop(0, ends - first, body, 0)
-        attend(i, 0, True)
-        if i:
-            @pl.when(low < 2)
-            def _():
-                give_back(0, 1, 1, device(x, across, y))
+        if dx == 0:
+            top[...] = high[:, 0:BLK]
+            total[...] = part[:, 0:BLK]
+            acc[...] = numer[:, 0:BLK]
+        for k in range(MATES):
+            if (dx, k) == (0, 0):
+                continue
+            slot = dx * MATES + k
+            lanes = slice(k * BLK, (k + 1) * BLK)
+            pout[slot] = (numer[:, lanes] / part[:, lanes]).astype(jnp.bfloat16)
+            sout[slot, 0:4] = jnp.broadcast_to(high[:, lanes], (4, BLK))
+            sout[slot, 4:8] = jnp.broadcast_to(part[:, lanes], (4, BLK))
+
+    def serve(dx):
+        for k in range(MATES):
+            if (dx, k) != (0, 0):
+                @pl.when(hosts(dx, k))
+                def _():
+                    q_copy(dx, k).wait_recv()
+        attend(dx)
+        for k in range(MATES):
+            if (dx, k) != (0, 0):
+                @pl.when(hosts(dx, k))
+                def _():
+                    for copy in p_copies(dx * MATES + k, device((x + dx) % XN, mate_z[k], y)):
+                        copy.start()
 
     for d, to in row_peers:
         row_copy(d, to).wait_recv()
-    for dx, k in near + far:
-        @pl.when(hosts(dx, k))
-        def _():
-            q_copy(dx, k).wait_recv()
-    compute(0)
     for d, to in pair_peers:
         pair_copy(d, to).wait_recv()
-    compute(1)
+    serve(0)
+    for dx in (2, 3, 1):
+        @pl.when(x + dx < XN)
+        def _():
+            serve(dx)
 
     mine[4].wait()
     first_pick, second_pick = picks[0, 0, ctx], picks[0, 1, ctx]
-    for dx, k in [(0, 1), (0, 2), (0, 3)] + [(dx, k) for dx in (1, 3, 2) for k in range(MATES)]:
-        @pl.when(visits(dx, k))
-        def _():
-            slot = dx * MATES + k
+
+    def combine(dx, ks):
+        slots = [dx * MATES + k for k in ks]
+        theirs = []
+        for k, slot in zip(ks, slots):
             for copy in p_copies(slot, (ctx, head)):
                 copy.wait_recv()
-            theirs = sin[slot, 0:1]
+            score = sin[slot, 0:1]
             if (dx, k) != (0, 1):
                 which = 2 * (x - dx) + (half if k < 2 else 1 - half)
-                picked = (first_pick == which) | (second_pick == which)
-                theirs = jnp.where(picked, theirs, NEGATIVE)
-            ours = top[0, :, 0:BLK]
-            high = jnp.maximum(ours, theirs)
-            fade = jnp.exp2((ours - high) * RATE)
-            share = sin[slot, 4:5] * jnp.exp2((theirs - high) * RATE)
-            top[0, :, 0:BLK] = high
-            total[0, :, 0:BLK] = total[0, :, 0:BLK] * fade + share
-            acc[0, :, 0:BLK] = acc[0, :, 0:BLK] * fade + pin[slot].astype(jnp.float32) * share
-
-    att[0] = (acc[0, :, 0:BLK] / total[0, :, 0:BLK]).T.astype(jnp.bfloat16)
+                score = jnp.where((first_pick == which) | (second_pick == which), score, NEGATIVE)
+            theirs.append(score)
+        ours = top[...]
+        high = ours
+        for score in theirs:
+            high = jnp.maximum(high, score)
+        fade = jnp.exp2((ours - high) * RATE)
+        part = total[...] * fade
+        numer = acc[...] * fade
+        for score, slot in zip(theirs, slots):
+            share = sin[slot, 4:5] * jnp.exp2((score - high) * RATE)
+            part = part + share
+            numer = numer + pin[slot].astype(jnp.float32) * share
+        top[...] = high
+        total[...] = part
+        acc[...] = numer
+
+    for dx, ks in [(0, (1,)), (0, (2, 3)), (2, range(MATES)), (1, range(MATES)), (3, range(MATES))]:
+        @pl.when(visits(dx, ks[0]))
+        def _():
+            combine(dx, ks)
+
+    att[0] = (acc[...] / total[...]).T.astype(jnp.bfloat16)
     att_copy.start()
     mine[3].wait()
     w_copy.wait_recv()
@@ -232,7 +233,8 @@
         out_ref[:, columns] = jnp.dot(attended, weight, preferred_element_type=jnp.float32).astype(jnp.bfloat16)
         return carry
 
-    lax.fori_loop(0, COLS // wide, project, 0)
+    for n in range(COLS // wide):
+        project(n, 0)
 
     for d, to in row_peers:
         row_copy(d, to).wait_send()
@@ -271,9 +273,9 @@
             pltpu.VMEM((SLOTS, 8, BLK), f32),
             pltpu.VMEM((2, BLK, COLS), bf16),
             pltpu.VMEM((2, BLK, BLK), bf16),
-            pltpu.VMEM((SLOTS // 2, 1, 2 * BLK), f32),
-            pltpu.VMEM((SLOTS // 2, 1, 2 * BLK), f32),
-            pltpu.VMEM((SLOTS // 2, BLK, 2 * BLK), f32),
+            pltpu.VMEM((1, BLK), f32),
+            pltpu.VMEM((1, BLK), f32),
+            pltpu.VMEM((BLK, BLK), f32),
             pltpu.SemaphoreType.REGULAR,
             dma((5,)),
             dma((2, YN)),

time: 46.1 us -> 38.8 us (0.84)
  Pallas kernels: 43.9 us -> 36.7 us
    pallas_call x1, Pallas kernels: 43.9 us -> 36.7 us  [local(): pl.pallas_call(kernel, out_shape=jax.ShapeDtypeStruct((BLK, COLS), bf16),...]
where the time goes in v3:
time: 38.8 us; the launch traced here: 38.6 us
  Pallas kernels  36.7 us (95%)
  local copies, waits for them, and re-layouts  1.88 us (5%)
    pallas_call x1, Pallas kernels, local(): pl.pallas_call(kernel, out_shape=jax.ShapeDtypeStruct((BLK, COLS), bf16),...  36.7 us
    unnamed x1, local copies, waits for them, and re-layouts  1.88 us

profile of v3, /device:TPU:3, one launch (start us, length us, event | category | flops | bytes accessed | tf_op | source)
XLA Modules:
  0.0 38.6 jit_solution(15907216254990766401)
XLA Ops:
  0.0 36.7 %shard_map.55 = bf16[128,2048]{1,0:T(8,128)(2,1)} custom-call(bf16[128,128]{1,0:T(8,128)(2,1)} %q_hbm.1, bf16[128,128]{1,0:T(8,128)(2,1)} %k_hbm.1, bf16[128,128]{1,0:T(8,128)(2,1)} %v_hbm.1, s32[1,2,128]{2,1,0:T(2,128)} %bitcast.1, bf16[128,4096]{1,0:T(8,128)(2,1)} %w_hbm.1), custom_call_target="tpu_custom_call" | custom-call | flops 1073741824 | bytes 4194304 | tf_op jit(solution)/shard_map/pallas_call | solution.py:260
  36.7 1.9 %copy.7 = bf16[128,2048]{1,0:T(8,128)(2,1)} copy(bf16[128,2048]{1,0:T(8,128)(2,1)} %shard_map.55) | data formatting | bytes 1048576

commit v4 on v3

--- a/solution.py
+++ b/solution.py
@@ -55,9 +55,9 @@
         pltpu.make_async_copy(picks_hbm, picks, local_sem.at[4]),
     ]
     row_peers = [(d, device(x, z, (y + d) % YN)) for d in range(1, YN)]
-    pair_peers = [(d, device(x, pair_z, (y + d) % YN)) for d in range(YN)]
+    pair_peer = device(x, pair_z, y)
     x_peers = [device((x + d) % XN, z, y) for d in range(1, XN)]
-    greeted = [to for _, to in row_peers + pair_peers]
+    greeted = [to for _, to in row_peers] + [pair_peer]
     greeted += [device(x, mate_z[k], y) for k in range(1, MATES)] + x_peers + [(ctx, other)]
     barrier = pltpu.get_barrier_semaphore()
     for to in greeted:
@@ -81,11 +81,10 @@
     for to in x_peers:
         pl.semaphore_signal(x_sem, inc=1, device_id=to, device_id_type=MESH)
 
-    def row_copy(d, to):
-        return remote(kv.at[0, y], kv.at[0, y], kv_send.at[0, d], kv_recv.at[0, d], to)
-
-    def pair_copy(d, to):
-        return remote(kv.at[0, y], kv.at[1, y], kv_send.at[1, d], kv_recv.at[1, d], to)
+    def row_copy(i, d, to):
+        return remote(kv.at[i, y], kv.at[i, y], kv_send.at[i, d], kv_recv.at[i, d], to)
+
+    pair_copy = remote(kv.at[0, y], kv.at[1, y], kv_send.at[1, 0], kv_recv.at[1, 0], pair_peer)
 
     def q_copy(dx, k):
         slot = dx * MATES + k
@@ -114,10 +113,9 @@
     )
     att_copy = remote(att.at[0], att.at[1], h_send.at[1], h_recv.at[1], (ctx, other))
 
+    pair_copy.start()
     for d, to in row_peers:
-        row_copy(d, to).start()
-    for d, to in pair_peers:
-        pair_copy(d, to).start()
+        row_copy(0, d, to).start()
     near = [(0, k) for k in range(1, MATES)] + [(dx, 0) for dx in (2, 3, 1)]
     far = [(dx, k) for dx in (2, 3, 1) for k in range(1, MATES)]
     for dx, k in near:
@@ -130,6 +128,9 @@
         def _():
             q_copy(dx, k).start()
     w_copy.start()
+    pair_copy.wait_recv()
+    for d, to in row_peers:
+        row_copy(1, d, to).start()
 
     def attend(dx):
         queries = qbuf[pl.ds(dx * MATES, MATES)].reshape(MATES * BLK, BLK)
@@ -175,10 +176,9 @@
                     for copy in p_copies(dx * MATES + k, device((x + dx) % XN, mate_z[k], y)):
                         copy.start()
 
-    for d, to in row_peers:
-        row_copy(d, to).wait_recv()
-    for d, to in pair_peers:
-        pair_copy(d, to).wait_recv()
+    for i in range(2):
+        for d, to in row_peers:
+            row_copy(i, d, to).wait_recv()
     serve(0)
     for dx in (2, 3, 1):
         @pl.when(x + dx < XN)
@@ -236,10 +236,10 @@
     for n in range(COLS // wide):
         project(n, 0)
 
-    for d, to in row_peers:
-        row_copy(d, to).wait_send()
-    for d, to in pair_peers:
-        pair_copy(d, to).wait_send()
+    pair_copy.wait_send()
+    for i in range(2):
+        for d, to in row_peers:
+            row_copy(i, d, to).wait_send()
     for dx, k in near + far:
         @pl.when(visits(dx, k))
         def _():

time: 38.8 us -> 37.5 us (0.966)
  Pallas kernels: 36.7 us -> 35.4 us
    pallas_call x1, Pallas kernels: 36.7 us -> 35.4 us  [local(): pl.pallas_call(kernel, out_shape=jax.ShapeDtypeStruct((BLK, COLS), bf16),...]
where the time goes in v4:
time: 37.5 us; the launch traced here: 37.3 us
  Pallas kernels  35.4 us (94%)
  local copies, waits for them, and re-layouts  1.88 us (5%)
    pallas_call x1, Pallas kernels, local(): pl.pallas_call(kernel, out_shape=jax.ShapeDtypeStruct((BLK, COLS), bf16),...  35.4 us
    unnamed x1, local copies, waits for them, and re-layouts  1.88 us

profile of v4, /device:TPU:3, one launch (start us, length us, event | category | flops | bytes accessed | tf_op | source)
XLA Modules:
  0.0 37.3 jit_solution(17633506542682726663)
XLA Ops:
  0.0 35.4 %shard_map.55 = bf16[128,2048]{1,0:T(8,128)(2,1)} custom-call(bf16[128,128]{1,0:T(8,128)(2,1)} %q_hbm.1, bf16[128,128]{1,0:T(8,128)(2,1)} %k_hbm.1, bf16[128,128]{1,0:T(8,128)(2,1)} %v_hbm.1, s32[1,2,128]{2,1,0:T(2,128)} %bitcast.1, bf16[128,4096]{1,0:T(8,128)(2,1)} %w_hbm.1), custom_call_target="tpu_custom_call" | custom-call | flops 1073741824 | bytes 4194304 | tf_op jit(solution)/shard_map/pallas_call | solution.py:260
  35.5 1.9 %copy.7 = bf16[128,2048]{1,0:T(8,128)(2,1)} copy(bf16[128,2048]{1,0:T(8,128)(2,1)} %shard_map.55) | data formatting | bytes 1048576

commit v5 on v4

--- a/solution.py
+++ b/solution.py
@@ -116,8 +116,8 @@
     pair_copy.start()
     for d, to in row_peers:
         row_copy(0, d, to).start()
-    near = [(0, k) for k in range(1, MATES)] + [(dx, 0) for dx in (2, 3, 1)]
-    far = [(dx, k) for dx in (2, 3, 1) for k in range(1, MATES)]
+    near = [(dx, 0) for dx in (2, 3, 1)] + [(0, k) for k in (3, 2, 1)]
+    far = [(dx, k) for k in (3, 2, 1) for dx in (2, 3, 1)]
     for dx, k in near:
         @pl.when(visits(dx, k))
         def _():
@@ -179,11 +179,11 @@
     for i in range(2):
         for d, to in row_peers:
             row_copy(i, d, to).wait_recv()
+    for dx in (1, 2, 3):
+        @pl.when(x + dx < XN)
+        def _():
+            serve(dx)
     serve(0)
-    for dx in (2, 3, 1):
-        @pl.when(x + dx < XN)
-        def _():
-            serve(dx)
 
     mine[4].wait()
     first_pick, second_pick = picks[0, 0, ctx], picks[0, 1, ctx]
@@ -259,7 +259,7 @@
     bf16, f32 = jnp.bfloat16, jnp.float32
     return pl.pallas_call(
         kernel,
-        out_shape=jax.ShapeDtypeStruct((BLK, COLS), bf16),
+        out_shape=pltpu.VMEM((BLK, COLS), bf16),
         in_specs=[hbm] * 5,
         out_specs=pl.BlockSpec(memory_space=pltpu.VMEM),
         scratch_shapes=[

time: 37.5 us -> 33.3 us (0.89)
  the two profiles are of different devices: /device:TPU:3 before, /device:TPU:7 now
where the time goes in v5:
time: 33.3 us; the launch traced here: 33.2 us
  Pallas kernels  32.4 us (97%)
  local copies, waits for them, and re-layouts  0.8 us (2%)
    pallas_call x1, Pallas kernels, local(): pl.pallas_call(kernel, out_shape=pltpu.VMEM((BLK, COLS), bf16), in_specs=...  32.4 us
    unnamed x1, local copies, waits for them, and re-layouts  0.8 us

profile of v5, /device:TPU:7, one launch (start us, length us, event | category | flops | bytes accessed | tf_op | source)
XLA Modules:
  0.0 33.2 jit_solution(4199448760096695145)
XLA Ops:
  0.0 32.4 %shard_map.55 = bf16[128,2048]{1,0:T(8,128)(2,1)S(1)} custom-call(bf16[128,128]{1,0:T(8,128)(2,1)} %q_hbm.1, bf16[128,128]{1,0:T(8,128)(2,1)} %k_hbm.1, bf16[128,128]{1,0:T(8,128)(2,1)} %v_hbm.1, s32[1,2,128]{2,1,0:T(2,128)} %bitcast.1, bf16[128,4096]{1,0:T(8,128)(2,1)} %w_hbm.1), custom_call_target="tpu_custom_call" | custom-call | flops 1073741824 | bytes 4194304 | tf_op jit(solution)/shard_map/pallas_call | solution.py:260
  32.4 0.8 %copy.7 = bf16[128,2048]{1,0:T(8,128)(2,1)} copy(bf16[128,2048]{1,0:T(8,128)(2,1)S(1)} %shard_map.55) | data formatting | bytes 1048576

commit v6 on v5

v6 whole, which is shorter than its diff:
```python
import math

import jax
import jax.numpy as jnp
from jax import lax
from jax.experimental import pallas as pl
from jax.experimental.pallas import tpu as pltpu
from jax.sharding import PartitionSpec as P

BLK = 128
XN = 4
YN = 4
ZN = 8
MATES = 4
NEAR = (3, 1, 2)
FORWARD = (2, 3, 1)
SERVE = (3, 1, 2, 0)
SLOTS = MATES * XN
CHUNK = YN * BLK
COLS = 2048
NEGATIVE = -1e30
RATE = math.log2(math.e) / math.sqrt(128.0)
MESH = pl.DeviceIdType.MESH


def kernel(
    q_hbm, k_hbm, v_hbm, picks_hbm, w_hbm, out_ref,
    picks, kv, qbuf, vraw, pout, sout, pin, sin, wbuf, att, top, total, acc,
    local_sem, kv_send, kv_recv, q_send, q_recv, p_send, p_recv, h_send, h_recv,
):
    ctx = lax.axis_index("ctx")
    head = lax.axis_index("head")
    x = ctx // 32
    z = (ctx % 32) // 4
    y = ctx % 4
    span = 2 * x + z // 4
    side = 1 - 2 * (z % 2)
    pair_z = z + side
    host_z = [z, (z + ZN + 2 * side) % ZN, (z + ZN - side) % ZN, (z + ZN - 3 * side) % ZN]
    guest_z = [z, (z + ZN - 2 * side) % ZN, host_z[2], host_z[3]]
    other = 1 - head

    def device(to_x, to_z, to_y):
        return (to_x * 32 + to_z * 4 + to_y, head)

    def remote(src, dst, send, recv, to):
        return pltpu.make_async_remote_copy(
            src_ref=src, dst_ref=dst, send_sem=send, recv_sem=recv, device_id=to, device_id_type=MESH
        )

    mine = [
        pltpu.make_async_copy(v_hbm, vraw, local_sem.at[0]),
        pltpu.make_async_copy(k_hbm, kv.at[0, y, pl.ds(0, BLK)], local_sem.at[1]),
        pltpu.make_async_copy(q_hbm, qbuf.at[0], local_sem.at[2]),
        pltpu.make_async_copy(
            w_hbm.at[:, pl.ds(pl.multiple_of(head * COLS, COLS), COLS)], wbuf.at[0], local_sem.at[3]
        ),
        pltpu.make_async_copy(picks_hbm, picks, local_sem.at[4]),
    ]
    row_peers = [(d, device(x, z, (y + d) % YN)) for d in range(1, YN)]
    pair_peer = device(x, pair_z, y)
    x_peers = [device((x + d) % XN, z, y) for d in range(1, XN)]
    greeted = [to for _, to in row_peers] + [pair_peer]
    greeted += [device(x, to_z, y) for to_z in host_z[1:] + guest_z[1:2]] + x_peers + [(ctx, other)]
    barrier = pltpu.get_barrier_semaphore()
    for to in greeted:
        pl.semaphore_signal(barrier, inc=1, device_id=to, device_id_type=MESH)
    for copy in mine:
        copy.start()

    def visits(dx, k):
        return x >= dx if dx else host_z[k] // 2 < z // 2

    def hosts(dx, k):
        return x + dx < XN if dx else z // 2 < guest_z[k] // 2

    for dx in range(XN):
        for k in range(MATES):
            if dx or k:
                @pl.when(jnp.logical_not(hosts(dx, k) if dx else (x >= 1) | hosts(0, k)))
                def _():
                    qbuf[k * XN + dx] = jnp.zeros((BLK, BLK), jnp.bfloat16)

    mine[0].wait()
    kv[0, y, BLK:] = vraw[...].T
    mine[1].wait()
    mine[2].wait()
    pl.semaphore_wait(barrier, len(greeted))

    def row_copy(i, d, to):
        return remote(kv.at[i, y], kv.at[i, y], kv_send.at[i, d], kv_recv.at[i, d], to)

    pair_copy = remote(kv.at[0, y], kv.at[1, y], kv_send.at[1, 0], kv_recv.at[1, 0], pair_peer)

    def z_copy(k):
        slot = k * XN
        return remote(qbuf.at[0], qbuf.at[slot], q_send.at[slot], q_recv.at[slot], device(x, host_z[k], y))

    def q_copy(dx, k):
        slot = k * XN + dx
        to = device((x + XN - dx) % XN, z, y)
        return remote(qbuf.at[k * XN], qbuf.at[slot], q_send.at[slot], q_recv.at[slot], to)

    def p_copies(slot, to):
        return [
            remote(pout.at[slot], pin.at[slot], p_send.at[slot, 0], p_recv.at[slot, 0], to),
            remote(sout.at[slot], sin.at[slot], p_send.at[slot, 1], p_recv.at[slot, 1], to),
        ]

    w_copy = remote(
        w_hbm.at[:, pl.ds(pl.multiple_of(other * COLS, COLS), COLS)],
        wbuf.at[1], h_send.at[0], h_recv.at[0], (ctx, other),
    )
    att_copy = remote(att.at[0], att.at[1], h_send.at[1], h_recv.at[1], (ctx, other))

    pair_copy.start()
    for d, to in row_peers:
        row_copy(0, d, to).start()
    for k in NEAR:
        @pl.when((x >= 1) | visits(0, k))
        def _():
            z_copy(k).start()
    for dx in FORWARD:
        @pl.when(x >= dx)
        def _():
            q_copy(dx, 0).start()
    w_copy.start()

    def forward(k):
        @pl.when((x >= 1) | hosts(0, k))
        def _():
            z_copy(k).wait_recv()
        for dx in FORWARD:
            @pl.when(x >= dx)
            def _():
                q_copy(dx, k).start()

    pair_copy.wait_recv()
    for d, to in row_peers:
        row_copy(1, d, to).start()
    forward(NEAR[0])
    for k in NEAR[1:]:
        forward(k)

    def attend(k):
        queries = qbuf[k * XN:(k + 1) * XN].reshape(XN * BLK, BLK)
        keys = jnp.concatenate([kv[i, :, 0:BLK].reshape(CHUNK, BLK) for i in range(2)], axis=0)
        scores = lax.dot_general(
            keys, queries, (((1,), (1,)), ((), ())), preferred_element_type=jnp.float32
        )
        if k == 0:
            key = lax.broadcasted_iota(jnp.int32, (2 * CHUNK, BLK), 0)
            token = lax.broadcasted_iota(jnp.int32, (2 * CHUNK, BLK), 1)
            last = jnp.where(key < CHUNK, y * BLK + token, jnp.where(pair_z < z, 2 * CHUNK, -1))
            own = jnp.where(key <= last, scores[:, 0:BLK], NEGATIVE)
            scores = jnp.concatenate([own, scores[:, BLK:]], axis=1)
        high = jnp.max(scores, axis=0, keepdims=True)
        weights = jnp.exp2((scores - high) * RATE)
        part = jnp.sum(weights, axis=0, keepdims=True)
        values = jnp.concatenate([kv[i, b, BLK:] for i in range(2) for b in range(YN)], axis=1)
        numer = jnp.dot(values, weights.astype(jnp.bfloat16), preferred_element_type=jnp.float32)
        if k == 0:
            top[...] = high[:, 0:BLK]
            total[...] = part[:, 0:BLK]
            acc[...] = numer[:, 0:BLK]
        for dx in range(XN):
            if (dx, k) == (0, 0):
                continue
            slot = k * XN + dx
            lanes = slice(dx * BLK, (dx + 1) * BLK)
            pout[slot] = (numer[:, lanes] / part[:, lanes]).astype(jnp.bfloat16)
            sout[slot, 0:1] = high[:, lanes]
            sout[slot, 1:2] = part[:, lanes]

    def serve(k):
        for dx in range(1, XN):
            @pl.when(hosts(dx, k))
            def _():
                q_copy(dx, k).wait_recv()
        attend(k)
        for dx in (2, 3, 1, 0):
            if (dx, k) != (0, 0):
                @pl.when(hosts(dx, k))
                def _():
                    for copy in p_copies(k * XN + dx, device((x + dx) % XN, guest_z[k], y)):
                        copy.start()

    for i in range(2):
        for d, to in row_peers:
            row_copy(i, d, to).wait_recv()
    for k in SERVE:
        @pl.when((x + 1 < XN) | hosts(0, k) if k else x >= 0)
        def _():
            serve(k)

    mine[4].wait()
    first_pick, second_pick = picks[0, 0, ctx], picks[0, 1, ctx]

    def combine(k, dxs):
        slots = [k * XN + dx for dx in dxs]
        theirs = []
        for dx, slot in zip(dxs, slots):
            for copy in p_copies(slot, (ctx, head)):
                copy.wait_recv()
            score = sin[slot, 0:1]
            which = 2 * (x - dx) + host_z[k] // 4
            wanted = (first_pick == which) | (second_pick == which) | (which == span)
            theirs.append(jnp.where(wanted, score, NEGATIVE))
        ours = top[...]
        high = ours
        for score in theirs:
            high = jnp.maximum(high, score)
        fade = jnp.exp2((ours - high) * RATE)
        part = total[...] * fade
        numer = acc[...] * fade
        for score, slot in zip(theirs, slots):
            share = sin[slot, 1:2] * jnp.exp2((score - high) * RATE)
            part = part + share
            numer = numer + pin[slot].astype(jnp.float32) * share
        top[...] = high
        total[...] = part
        acc[...] = numer

    for k in SERVE:
        if k:
            @pl.when(visits(0, k))
            def _():
                combine(k, [0])

        for far_x in range(1, XN):
            @pl.when(x == far_x)
            def _():
                combine(k, range(1, far_x + 1))

    att[0] = (acc[...] / total[...]).T.astype(jnp.bfloat16)
    att_copy.start()
    mine[3].wait()
    w_copy.wait_recv()
    att_copy.wait_recv()
    attended = jnp.concatenate([att[0], att[1]], axis=1)
    wide = 512

    def project(n, carry):
        columns = pl.ds(pl.multiple_of(n * wide, wide), wide)
        weight = wbuf[:, :, columns].reshape(2 * BLK, wide)
        out_ref[:, columns] = jnp.dot(attended, weight, preferred_element_type=jnp.float32).astype(jnp.bfloat16)
        return carry

    for n in range(COLS // wide):
        project(n, 0)

    pair_copy.wait_send()
    for i in range(2):
        for d, to in row_peers:
            row_copy(i, d, to).wait_send()
    for k in range(MATES):
        for dx in range(XN):
            if dx:
                @pl.when(x >= dx)
                def _():
                    q_copy(dx, k).wait_send()
            elif k:
                @pl.when((x >= 1) | visits(0, k))
                def _():
                    z_copy(k).wait_send()
            if dx or k:
                @pl.when(hosts(dx, k))
                def _():
                    for copy in p_copies(k * XN + dx, device((x + dx) % XN, guest_z[k], y)):
                        copy.wait_send()
    w_copy.wait_send()
    att_copy.wait_send()


def local(queries, keys, values, picks, out_weight):
    hbm = pl.BlockSpec(memory_space=pltpu.HBM)
    dma = pltpu.SemaphoreType.DMA
    bf16, f32 = jnp.bfloat16, jnp.float32
    return pl.pallas_call(
        kernel,
        out_shape=pltpu.VMEM((BLK, COLS), bf16),
        in_specs=[hbm] * 5,
        out_specs=pl.BlockSpec(memory_space=pltpu.VMEM),
        scratch_shapes=[
            pltpu.SMEM((1, 2, BLK), jnp.int32),
            pltpu.VMEM((2, YN, 2 * BLK, BLK), bf16),
            pltpu.VMEM((SLOTS, BLK, BLK), bf16),
            pltpu.VMEM((BLK, BLK), bf16),
            pltpu.VMEM((SLOTS, BLK, BLK), bf16),
            pltpu.VMEM((SLOTS, 2, BLK), f32),
            pltpu.VMEM((SLOTS, BLK, BLK), bf16),
            pltpu.VMEM((SLOTS, 2, BLK), f32),
            pltpu.VMEM((2, BLK, COLS), bf16),
            pltpu.VMEM((2, BLK, BLK), bf16),
            pltpu.VMEM((1, BLK), f32),
            pltpu.VMEM((1, BLK), f32),
            pltpu.VMEM((BLK, BLK), f32),
            dma((5,)),
            dma((2, YN)),
            dma((2, YN)),
            dma((SLOTS,)),
            dma((SLOTS,)),
            dma((SLOTS, 2)),
            dma((SLOTS, 2)),
            dma((2,)),
            dma((2,)),
        ],
        compiler_params=pltpu.CompilerParams(
            collective_id=0, has_side_effects=True, vmem_limit_bytes=56 * 1024 * 1024
        ),
        cost_estimate=pl.CostEstimate(flops=2**30, bytes_accessed=2**22, transcendentals=2**21),
    )(queries, keys, values, jnp.swapaxes(picks, 1, 2), out_weight)


def solution(mesh):
    placed = (
        P("ctx", "head"),
        P("ctx", "head"),
        P("ctx", "head"),
        P("head", None, None),
        P("head", None),
    )
    return jax.shard_map(
        local, mesh=mesh, in_specs=placed, out_specs=P("ctx", "head"), check_vma=False
    )
```

time: 33.3 us -> 31.3 us (0.940)
  the two profiles are of different devices: /device:TPU:7 before, /device:TPU:3 now
where the time goes in v6:
time: 31.3 us
  Pallas kernels  30.5 us (97%)
  local copies, waits for them, and re-layouts  0.8 us (3%)
    pallas_call x1, Pallas kernels, local(): pl.pallas_call(kernel, out_shape=pltpu.VMEM((BLK, COLS), bf16), in_specs=...  30.5 us
    unnamed x1, local copies, waits for them, and re-layouts  0.8 us

profile of v6, /device:TPU:3, one launch (start us, length us, event | category | flops | bytes accessed | tf_op | source)
XLA Modules:
  0.0 31.3 jit_solution(12119341416206046426)
XLA Ops:
  0.0 30.5 %shard_map.55 = bf16[128,2048]{1,0:T(8,128)(2,1)S(1)} custom-call(bf16[128,128]{1,0:T(8,128)(2,1)} %q_hbm.1, bf16[128,128]{1,0:T(8,128)(2,1)} %k_hbm.1, bf16[128,128]{1,0:T(8,128)(2,1)} %v_hbm.1, s32[1,2,128]{2,1,0:T(2,128)} %bitcast.1, bf16[128,4096]{1,0:T(8,128)(2,1)} %w_hbm.1), custom_call_target="tpu_custom_call" | custom-call | flops 1073741824 | bytes 4194304 | tf_op jit(solution)/shard_map/pallas_call | solution.py:279
  30.5 0.8 %copy.7 = bf16[128,2048]{1,0:T(8,128)(2,1)} copy(bf16[128,2048]{1,0:T(8,128)(2,1)S(1)} %shard_map.55) | data formatting | bytes 1048576

commit v7 on v6

--- a/solution.py
+++ b/solution.py
@@ -13,7 +13,7 @@
 ZN = 8
 MATES = 4
 NEAR = (3, 1, 2)
-FORWARD = (2, 3, 1)
+FORWARD = (3, 2, 1)
 SERVE = (3, 1, 2, 0)
 SLOTS = MATES * XN
 CHUNK = YN * BLK
@@ -25,7 +25,7 @@
 
 def kernel(
     q_hbm, k_hbm, v_hbm, picks_hbm, w_hbm, out_ref,
-    picks, kv, qbuf, vraw, pout, sout, pin, sin, wbuf, att, top, total, acc,
+    picks, kv, qbuf, vraw, pout, sout, pin, sin, wbuf, att, term, top, total, acc,
     local_sem, kv_send, kv_recv, q_send, q_recv, p_send, p_recv, h_send, h_recv,
 ):
     ctx = lax.axis_index("ctx")
@@ -38,6 +38,8 @@
     pair_z = z + side
     host_z = [z, (z + ZN + 2 * side) % ZN, (z + ZN - side) % ZN, (z + ZN - 3 * side) % ZN]
     guest_z = [z, (z + ZN - 2 * side) % ZN, host_z[2], host_z[3]]
+    middle = (z == 1) | (z == 2)
+    edge = (z == 0) | (z == 3)
     other = 1 - head
 
     def device(to_x, to_z, to_y):
@@ -57,7 +59,7 @@
         ),
         pltpu.make_async_copy(picks_hbm, picks, local_sem.at[4]),
     ]
-    row_peers = [(d, device(x, z, (y + d) % YN)) for d in range(1, YN)]
+    row_peers = [(d, device(x, z, (y + d) % YN)) for d in (2, 1, 3)]
     pair_peer = device(x, pair_z, y)
     x_peers = [device((x + d) % XN, z, y) for d in range(1, XN)]
     greeted = [to for _, to in row_peers] + [pair_peer]
@@ -87,10 +89,21 @@
     mine[2].wait()
     pl.semaphore_wait(barrier, len(greeted))
 
-    def row_copy(i, d, to):
-        return remote(kv.at[i, y], kv.at[i, y], kv_send.at[i, d], kv_recv.at[i, d], to)
-
-    pair_copy = remote(kv.at[0, y], kv.at[1, y], kv_send.at[1, 0], kv_recv.at[1, 0], pair_peer)
+    def row_copy(d, to):
+        return remote(kv.at[0, y], kv.at[0, y], kv_send.at[0, d], kv_recv.at[0, d], to)
+
+    def pair_copy(part):
+        rows = pl.ds(part * BLK, BLK)
+        return remote(
+            kv.at[0, y, rows], kv.at[1, y, rows], kv_send.at[part, 0], kv_recv.at[part, 0], pair_peer
+        )
+
+    def onward_copy(part, d, to):
+        rows = pl.ds(part * BLK, BLK)
+        at = kv.at[1, y, rows]
+        return remote(at, at, kv_send.at[1 + part, d], kv_recv.at[1 + part, d], to)
+
+    onward = [(part, d, to) for part in range(2) for d, to in row_peers]
 
     def z_copy(k):
         slot = k * XN
@@ -113,9 +126,10 @@
     )
     att_copy = remote(att.at[0], att.at[1], h_send.at[1], h_recv.at[1], (ctx, other))
 
-    pair_copy.start()
+    for part in range(2):
+        pair_copy(part).start()
     for d, to in row_peers:
-        row_copy(0, d, to).start()
+        row_copy(d, to).start()
     for k in NEAR:
         @pl.when((x >= 1) | visits(0, k))
         def _():
@@ -135,9 +149,10 @@
             def _():
                 q_copy(dx, k).start()
 
-    pair_copy.wait_recv()
-    for d, to in row_peers:
-        row_copy(1, d, to).start()
+    for part in range(2):
+        pair_copy(part).wait_recv()
+        for d, to in row_peers:
+            onward_copy(part, d, to).start()
     forward(NEAR[0])
     for k in NEAR[1:]:
         forward(k)
@@ -185,11 +200,13 @@
                     for copy in p_copies(k * XN + dx, device((x + dx) % XN, guest_z[k], y)):
                         copy.start()
 
-    for i in range(2):
-        for d, to in row_peers:
-            row_copy(i, d, to).wait_recv()
-    for k in SERVE:
-        @pl.when((x + 1 < XN) | hosts(0, k) if k else x >= 0)
+    for d, to in row_peers:
+        row_copy(d, to).wait_recv()
+    for hop in onward:
+        onward_copy(*hop).wait_recv()
+    turns = [(0, edge), (3, jnp.logical_not(middle)), (1, x >= 0), (2, x >= 0), (0, jnp.logical_not(edge)), (3, middle)]
+    for k, now in turns:
+        @pl.when(now & ((x + 1 < XN) | hosts(0, k)) if k else now)
         def _():
             serve(k)
 
@@ -236,23 +253,21 @@
     att_copy.start()
     mine[3].wait()
     w_copy.wait_recv()
+    wide = 512
+    columns = [slice(n, n + wide) for n in range(0, COLS, wide)]
+    for part in columns:
+        term[:, part] = jnp.dot(att[0], wbuf[0, :, part], preferred_element_type=jnp.float32)
     att_copy.wait_recv()
-    attended = jnp.concatenate([att[0], att[1]], axis=1)
-    wide = 512
-
-    def project(n, carry):
-        columns = pl.ds(pl.multiple_of(n * wide, wide), wide)
-        weight = wbuf[:, :, columns].reshape(2 * BLK, wide)
-        out_ref[:, columns] = jnp.dot(attended, weight, preferred_element_type=jnp.float32).astype(jnp.bfloat16)
-        return carry
-
-    for n in range(COLS // wide):
-        project(n, 0)
-
-    pair_copy.wait_send()
-    for i in range(2):
-        for d, to in row_peers:
-            row_copy(i, d, to).wait_send()
+    for part in columns:
+        more = jnp.dot(att[1], wbuf[1, :, part], preferred_element_type=jnp.float32)
+        out_ref[:, part] = (term[:, part] + more).astype(jnp.bfloat16)
+
+    for part in range(2):
+        pair_copy(part).wait_send()
+    for d, to in row_peers:
+        row_copy(d, to).wait_send()
+    for hop in onward:
+        onward_copy(*hop).wait_send()
     for k in range(MATES):
         for dx in range(XN):
             if dx:
@@ -292,12 +307,13 @@
             pltpu.VMEM((SLOTS, 2, BLK), f32),
             pltpu.VMEM((2, BLK, COLS), bf16),
             pltpu.VMEM((2, BLK, BLK), bf16),
+            pltpu.VMEM((BLK, COLS), f32),
             pltpu.VMEM((1, BLK), f32),
             pltpu.VMEM((1, BLK), f32),
             pltpu.VMEM((BLK, BLK), f32),
             dma((5,)),
-            dma((2, YN)),
-            dma((2, YN)),
+            dma((3, YN)),
+            dma((3, YN)),
             dma((SLOTS,)),
             dma((SLOTS,)),
             dma((SLOTS, 2)),

time: 31.3 us -> 31.1 us (level)
  Pallas kernels: 30.5 us -> 30.1 us
    pallas_call x1, Pallas kernels: 30.5 us -> 30.1 us  [local(): pl.pallas_call(kernel, out_shape=pltpu.VMEM((BLK, COLS), bf16), in_specs=...]
where the time goes in v7:
time: 31.1 us; the launch traced here: 30.9 us
  Pallas kernels  30.1 us (97%)
  local copies, waits for them, and re-layouts  0.8 us (3%)
    pallas_call x1, Pallas kernels, local(): pl.pallas_call(kernel, out_shape=pltpu.VMEM((BLK, COLS), bf16), in_specs=...  30.1 us
    unnamed x1, local copies, waits for them, and re-layouts  0.8 us

profile of v7, /device:TPU:3, one launch (start us, length us, event | category | flops | bytes accessed | tf_op | source)
XLA Modules:
  0.0 30.9 jit_solution(12770491990855244648)
XLA Ops:
  0.0 30.1 %shard_map.55 = bf16[128,2048]{1,0:T(8,128)(2,1)S(1)} custom-call(bf16[128,128]{1,0:T(8,128)(2,1)} %q_hbm.1, bf16[128,128]{1,0:T(8,128)(2,1)} %k_hbm.1, bf16[128,128]{1,0:T(8,128)(2,1)} %v_hbm.1, s32[1,2,128]{2,1,0:T(2,128)} %bitcast.1, bf16[128,4096]{1,0:T(8,128)(2,1)} %w_hbm.1), custom_call_target="tpu_custom_call" | custom-call | flops 1073741824 | bytes 4194304 | tf_op jit(solution)/shard_map/pallas_call | solution.py:294
  30.1 0.8 %copy.7 = bf16[128,2048]{1,0:T(8,128)(2,1)} copy(bf16[128,2048]{1,0:T(8,128)(2,1)S(1)} %shard_map.55) | data formatting | bytes 1048576

commit v8 on v7

--- a/solution.py
+++ b/solution.py
@@ -178,7 +178,7 @@
             top[...] = high[:, 0:BLK]
             total[...] = part[:, 0:BLK]
             acc[...] = numer[:, 0:BLK]
-        for dx in range(XN):
+        for dx in (2, 3, 1, 0):
             if (dx, k) == (0, 0):
                 continue
             slot = k * XN + dx
@@ -187,18 +187,17 @@
             sout[slot, 0:1] = high[:, lanes]
             sout[slot, 1:2] = part[:, lanes]
 
+            @pl.when(hosts(dx, k))
+            def _():
+                for copy in p_copies(slot, device((x + dx) % XN, guest_z[k], y)):
+                    copy.start()
+
     def serve(k):
         for dx in range(1, XN):
             @pl.when(hosts(dx, k))
             def _():
                 q_copy(dx, k).wait_recv()
         attend(k)
-        for dx in (2, 3, 1, 0):
-            if (dx, k) != (0, 0):
-                @pl.when(hosts(dx, k))
-                def _():
-                    for copy in p_copies(k * XN + dx, device((x + dx) % XN, guest_z[k], y)):
-                        copy.start()
 
     for d, to in row_peers:
         row_copy(d, to).wait_recv()

time: 31.1 us -> 30.9 us (level)
  no operation moved by 1% of the time
where the time goes in v8:
time: 30.9 us; the launch traced here: 30.8 us
  Pallas kernels  30 us (97%)
  local copies, waits for them, and re-layouts  0.8 us (3%)
    pallas_call x1, Pallas kernels, local(): pl.pallas_call(kernel, out_shape=pltpu.VMEM((BLK, COLS), bf16), in_specs=...  30 us
    unnamed x1, local copies, waits for them, and re-layouts  0.8 us

profile of v8, /device:TPU:3, one launch (start us, length us, event | category | flops | bytes accessed | tf_op | source)
XLA Modules:
  0.0 30.8 jit_solution(13884101362053245029)
XLA Ops:
  0.0 30.0 %shard_map.55 = bf16[128,2048]{1,0:T(8,128)(2,1)S(1)} custom-call(bf16[128,128]{1,0:T(8,128)(2,1)} %q_hbm.1, bf16[128,128]{1,0:T(8,128)(2,1)} %k_hbm.1, bf16[128,128]{1,0:T(8,128)(2,1)} %v_hbm.1, s32[1,2,128]{2,1,0:T(2,128)} %bitcast.1, bf16[128,4096]{1,0:T(8,128)(2,1)} %w_hbm.1), custom_call_target="tpu_custom_call" | custom-call | flops 1073741824 | bytes 4194304 | tf_op jit(solution)/shard_map/pallas_call | solution.py:293
  30.0 0.8 %copy.7 = bf16[128,2048]{1,0:T(8,128)(2,1)} copy(bf16[128,2048]{1,0:T(8,128)(2,1)S(1)} %shard_map.55) | data formatting | bytes 1048576

commit v9 on v7

--- a/solution.py
+++ b/solution.py
@@ -175,7 +175,7 @@
         values = jnp.concatenate([kv[i, b, BLK:] for i in range(2) for b in range(YN)], axis=1)
         numer = jnp.dot(values, weights.astype(jnp.bfloat16), preferred_element_type=jnp.float32)
         if k == 0:
-            top[...] = high[:, 0:BLK]
+            top[...] = high[:, 0:BLK] * RATE
             total[...] = part[:, 0:BLK]
             acc[...] = numer[:, 0:BLK]
         for dx in range(XN):
@@ -184,8 +184,7 @@
             slot = k * XN + dx
             lanes = slice(dx * BLK, (dx + 1) * BLK)
             pout[slot] = (numer[:, lanes] / part[:, lanes]).astype(jnp.bfloat16)
-            sout[slot, 0:1] = high[:, lanes]
-            sout[slot, 1:2] = part[:, lanes]
+            sout[slot] = high[:, lanes] * RATE + jnp.log2(part[:, lanes])
 
     def serve(k):
         for dx in range(1, XN):
@@ -227,11 +226,11 @@
         high = ours
         for score in theirs:
             high = jnp.maximum(high, score)
-        fade = jnp.exp2((ours - high) * RATE)
+        fade = jnp.exp2(ours - high)
         part = total[...] * fade
         numer = acc[...] * fade
         for score, slot in zip(theirs, slots):
-            share = sin[slot, 1:2] * jnp.exp2((score - high) * RATE)
+            share = jnp.exp2(score - high)
             part = part + share
             numer = numer + pin[slot].astype(jnp.float32) * share
         top[...] = high
@@ -302,9 +301,9 @@
             pltpu.VMEM((SLOTS, BLK, BLK), bf16),
             pltpu.VMEM((BLK, BLK), bf16),
             pltpu.VMEM((SLOTS, BLK, BLK), bf16),
-            pltpu.VMEM((SLOTS, 2, BLK), f32),
+            pltpu.VMEM((SLOTS, 1, BLK), f32),
             pltpu.VMEM((SLOTS, BLK, BLK), bf16),
-            pltpu.VMEM((SLOTS, 2, BLK), f32),
+            pltpu.VMEM((SLOTS, 1, BLK), f32),
             pltpu.VMEM((2, BLK, COLS), bf16),
             pltpu.VMEM((2, BLK, BLK), bf16),
             pltpu.VMEM((BLK, COLS), f32),

time: 31.1 us -> 31 us (level)
  no operation moved by 1% of the time
where the time goes in v9:
time: 31 us; the launch traced here: 30.9 us
  Pallas kernels  30.1 us (97%)
  local copies, waits for them, and re-layouts  0.8 us (3%)
    pallas_call x1, Pallas kernels, local(): pl.pallas_call(kernel, out_shape=pltpu.VMEM((BLK, COLS), bf16), in_specs=...  30.1 us
    unnamed x1, local copies, waits for them, and re-layouts  0.8 us

profile of v9, /device:TPU:3, one launch (start us, length us, event | category | flops | bytes accessed | tf_op | source)
XLA Modules:
  0.0 30.9 jit_solution(16511815065380018047)
XLA Ops:
  0.0 30.1 %shard_map.55 = bf16[128,2048]{1,0:T(8,128)(2,1)S(1)} custom-call(bf16[128,128]{1,0:T(8,128)(2,1)} %q_hbm.1, bf16[128,128]{1,0:T(8,128)(2,1)} %k_hbm.1, bf16[128,128]{1,0:T(8,128)(2,1)} %v_hbm.1, s32[1,2,128]{2,1,0:T(2,128)} %bitcast.1, bf16[128,4096]{1,0:T(8,128)(2,1)} %w_hbm.1), custom_call_target="tpu_custom_call" | custom-call | flops 1073741824 | bytes 4194304 | tf_op jit(solution)/shard_map/pallas_call | solution.py:293
  30.1 0.8 %copy.7 = bf16[128,2048]{1,0:T(8,128)(2,1)} copy(bf16[128,2048]{1,0:T(8,128)(2,1)S(1)} %shard_map.55) | data formatting | bytes 1048576
